TPU v7x, 32 devices: a whole 2x2x4 slice. The times are simulated.
32 devices in a mesh: cell: 8 (over y, x, core), gene: 4 (over z).
Axes of the slice: x: 2, y: 2, z: 4, core: 2. Of those that a mesh axis runs over, the one named last changes fastest.
Arguments:
- counts: bfloat16 [16384, 4096], P('cell', 'gene'), may hold values from -14 to 14
- loadings: bfloat16 [4096, 256], P('gene'), may hold values from -0.09375 to 0.09375
- kernel_widths: float32 [8], replicated, may hold values from 0.4 to 1.6
- width_index: int32 [16384], P(('cell', 'gene')), may hold values from 0 to 7
- block_fill: int32 [8], replicated, may hold values from 1 to 2048, 12288 in all
- plan: int32 [2], replicated, may hold values from 1 to 7, as said below
Outputs:
- density: float32 [16384], P(('cell', 'gene'))
- eccentricity: float32 [16384], P(('cell', 'gene'))
Inputs may be any that keep to these rules, and one draw needn't show every extreme that they name: `plan`: the 2 values are distinct and one of them is 7.
All inputs are finite; a program needn't handle non-finite values.
Results may differ from a plain program's by a relative error of at most 0.00031.
Values may be sent and summed in bfloat16 or wider, within the bound.
A program may use at most 64 MiB of HBM per device.

v0:
```python
import functools
import math
import jax
import jax.numpy as jnp
from jax import lax
from jax.experimental import pallas as pl
from jax.experimental.pallas import tpu as pltpu
from jax.sharding import PartitionSpec as P

MESH = pl.DeviceIdType.MESH
PIECE = 128
TILE = 256
FAR = 1e30


def flip(place, mask):
    for bit in range(mask.bit_length()):
        if (mask >> bit) & 1:
            place = place + (1 << bit) * (1 - 2 * (place // (1 << bit) % 2))
    return place


def remote(src, dst, send, recv, **device):
    return pltpu.make_async_remote_copy(
        src_ref=src, dst_ref=dst, send_sem=send, recv_sem=recv, device_id=device, device_id_type=MESH
    )


def kernel(
    cells,
    counts,
    loadings,
    index,
    widths,
    fills,
    plan,
    density,
    spread,
    held,
    wire,
    inbox,
    cross,
    whole,
    guests,
    coefs,
    outbox,
    results,
    near_norm,
    far_norm,
    held_sem,
    end_send,
    end_recv,
    mid_send,
    mid_recv,
    final_send,
    final_recv,
    over_send,
    over_recv,
    guest_send,
    guest_recv,
    pass_send,
    pass_recv,
    coef_send,
    coef_recv,
    result_send,
    result_recv,
):
    c, z = lax.axis_index("cell"), lax.axis_index("gene")
    rows, comps = whole.shape
    half = rows // 2
    steps = half // PIECE
    share = guests.shape[1]
    own_steps = share // PIECE
    side = z // 2
    is_mid = (z + 1) // 2 % 2 == 1
    is_end = (z + 1) // 2 % 2 == 0
    mate = z + 1 - 2 * (z % 2)
    opposite = 3 - z
    near, far = side * half, half - side * half
    own_first = z % 2 * own_steps
    relations = (1, 2, 4, 6)

    def part(base, i):
        return pl.ds(pl.multiple_of(base + i * PIECE, PIECE), PIECE)

    def held_copy(base, i, k):
        at = part(base, i)
        return pltpu.make_async_copy(counts.at[at], held.at[at], held_sem.at[2 * i + k])

    def end_copy(base, i, k):
        at = part(base, i)
        return remote(wire.at[at], inbox.at[at], end_send.at[2 * i + k], end_recv.at[2 * i + k], gene=mate)

    def mid_copy(base, i):
        at = part(base, i)
        return remote(wire.at[at], cross.at[at], mid_send.at[i], mid_recv.at[i], gene=opposite)

    def final_copy(base, i, k):
        at = part(base, i)
        return remote(whole.at[at], whole.at[at], final_send.at[2 * i + k], final_recv.at[2 * i + k], gene=mate)

    def over_copy(base, i):
        at = part(base, i)
        return remote(whole.at[at], whole.at[at], over_send.at[i], over_recv.at[i], gene=opposite)

    def guest_copy(r, i, slot):
        j = i - own_first
        return remote(
            whole.at[part(near, i)],
            guests.at[slot, part(0, j)],
            guest_send.at[r * own_steps + j],
            guest_recv.at[r * own_steps + j],
            cell=flip(c, relations[r]),
        )

    def pass_copy(r, j, slot):
        at = part(0, j)
        return remote(
            guests.at[slot, at],
            guests.at[slot, at],
            pass_send.at[(r - 1) * own_steps + j],
            pass_recv.at[(r - 1) * own_steps + j],
            cell=flip(c, 1),
        )

    def coef_copy(mask, slot):
        return remote(
            coefs.at[slot], coefs.at[slot], coef_send.at[mask - 1], coef_recv.at[mask - 1], cell=flip(c, mask)
        )

    def result_copy(mask, slot):
        return remote(
            outbox, results.at[slot], result_send.at[mask - 1], result_recv.at[mask - 1], cell=flip(c, mask)
        )

    def offer(i):
        @pl.when((i >= own_first) & (i < own_first + own_steps))
        def _():
            for r in range(4):
                guest_copy(r, i, c).start()

    def product(base, i, k):
        held_copy(base, i, k).wait()
        return jnp.dot(held[part(base, i), :], loadings[...], preferred_element_type=jnp.float32)

    def loop(count, body):
        def step(i, carry):
            body(i)
            return carry

        lax.fori_loop(0, count, step, 0)

    @functools.partial(loop, steps)
    def _(i):
        held_copy(far, i, 0).start()
        held_copy(near, i, 1).start()

    barrier = pltpu.get_barrier_semaphore()
    for mask in range(1, cells):
        pl.semaphore_signal(barrier, inc=1, device_id={"cell": flip(c, mask)}, device_id_type=MESH)
    pl.semaphore_signal(barrier, inc=1, device_id={"gene": mate}, device_id_type=MESH)

    @pl.when(is_mid)
    def _():
        pl.semaphore_signal(barrier, inc=1, device_id={"gene": opposite}, device_id_type=MESH)

    picked = jnp.zeros(index.shape, jnp.float32)
    for entry in range(widths.shape[0]):
        picked = picked + jnp.where(index[...] == entry, widths[entry], 0.0)
    own_coef = 1.0 / (2.0 * comps * picked * picked)
    coefs[c] = jnp.broadcast_to(own_coef, (8, share))

    @pl.when(is_end)
    def _():
        pl.semaphore_wait(barrier, cells)

        @functools.partial(loop, steps)
        def _(i):
            for k, base in enumerate((far, near)):
                wire[part(base, i), :] = product(base, i, k).astype(wire.dtype)
                end_copy(base, i, k).start()

        for mask in range(1, cells):
            coef_copy(mask, c).start()

        @functools.partial(loop, steps)
        def _(i):
            final_copy(near, i, 1).wait_recv()
            offer(i)
            final_copy(far, i, 0).wait_recv()

        @functools.partial(loop, steps)
        def _(i):
            end_copy(far, i, 0).wait_send()
            end_copy(near, i, 1).wait_send()

    @pl.when(is_mid)
    def _():
        pl.semaphore_wait(barrier, cells + 1)
        for mask in range(1, cells):
            coef_copy(mask, c).start()

        @functools.partial(loop, steps)
        def _(i):
            far_part = product(far, i, 0)
            near_part = product(near, i, 1)
            end_copy(far, i, 0).wait_recv()
            far_part = far_part + inbox[part(far, i), :].astype(jnp.float32)
            wire[part(far, i), :] = far_part.astype(wire.dtype)
            mid_copy(far, i).start()

            @pl.when(i > 0)
            def _():
                over_copy(far, i - 1).wait_recv()
                final_copy(far, i - 1, 0).start()

            end_copy(near, i, 1).wait_recv()
            near_part = near_part + inbox[part(near, i), :].astype(jnp.float32)
            mid_copy(near, i).wait_recv()
            near_part = near_part + cross[part(near, i), :].astype(jnp.float32)
            whole[part(near, i), :] = near_part.astype(whole.dtype)
            over_copy(near, i).start()
            final_copy(near, i, 1).start()
            offer(i)

        over_copy(far, steps - 1).wait_recv()
        final_copy(far, steps - 1, 0).start()

        @functools.partial(loop, steps)
        def _(i):
            mid_copy(far, i).wait_send()
            over_copy(near, i).wait_send()
            final_copy(near, i, 1).wait_send()
            final_copy(far, i, 0).wait_send()

    @functools.partial(loop, own_steps)
    def _(j):
        for r in range(1, 4):
            slot = flip(c, relations[r])
            guest_copy(r, own_first + j, slot).wait_recv()
            pass_copy(r, j, slot).start()

    fill = fills[c]

    @functools.partial(loop, rows // TILE)
    def _(t):
        at = pl.ds(pl.multiple_of(t * TILE, TILE), TILE)
        keys = whole[at, :].astype(jnp.float32)
        norm = jnp.sum(keys * keys, axis=1, keepdims=True)
        live = t * TILE + lax.broadcasted_iota(jnp.int32, (TILE, 1), 0) < fill
        near_norm[at, :] = jnp.broadcast_to(jnp.where(live, norm, FAR), (TILE, 128))
        far_norm[at, :] = jnp.broadcast_to(jnp.where(live, norm, -FAR), (TILE, 128))

    def dot_t(a, b):
        return lax.dot_general(a, b, (((1,), (1,)), ((), ())), preferred_element_type=jnp.float32)

    def terms(queries, coef):
        square = queries.astype(jnp.float32)
        square = square * square
        high = square.astype(jnp.bfloat16)
        low = (square - high.astype(jnp.float32)).astype(jnp.bfloat16)
        ones = jnp.ones((8, comps), jnp.bfloat16)
        norm = dot_t(ones, high) + dot_t(ones, low)
        rate = coef * (-1.0 / math.log(2.0))
        doubled = queries * jnp.asarray(-2.0, queries.dtype)

        def step(t, carry):
            total, top = carry
            at = pl.ds(pl.multiple_of(t * TILE, TILE), TILE)
            inner = dot_t(whole[at, :], doubled).reshape(TILE // 8, 8, share)
            closest = jnp.concatenate([near_norm[at, :].reshape(TILE // 8, 8, 128)] * (share // 128), axis=2)
            farthest = jnp.concatenate([far_norm[at, :].reshape(TILE // 8, 8, 128)] * (share // 128), axis=2)
            base = inner + norm[None]
            weight = jnp.exp2(jnp.maximum(base + closest, 0.0) * rate[None])
            total = total + jnp.sum(weight, axis=0)
            top = jnp.maximum(top, jnp.max(base + farthest, axis=0))
            return total, top

        zero = jnp.zeros((8, share), jnp.float32)
        total, top = lax.fori_loop(0, rows // TILE, step, (zero, zero))
        return jnp.sum(total, axis=0, keepdims=True), jnp.max(top, axis=0, keepdims=True)

    own_rows = pl.ds(pl.multiple_of(z * share, share), share)
    total, top = terms(whole[own_rows, :], coefs[c])

    @functools.partial(loop, own_steps)
    def _(j):
        guest_copy(0, own_first + j, flip(c, 1)).wait_recv()
        for r in range(1, 4):
            pass_copy(r, j, flip(c, relations[r] + 1)).wait_recv()

    for mask in range(1, cells):
        coef_copy(mask, flip(c, mask)).wait_recv()

    opposite_cell = flip(c, cells - 1)
    other_cell = jnp.bitwise_and(jnp.bitwise_xor(c, plan[0] + plan[1] - (cells - 1)), cells - 1)
    for at, guest in ((0, opposite_cell), (2, other_cell)):
        more, most = terms(guests[guest], coefs[guest])
        outbox[at : at + 1, :] = more
        outbox[at + 1 : at + 2, :] = most
    outbox[4:8, :] = jnp.zeros((4, share), jnp.float32)
    for mask in range(1, cells):
        result_copy(mask, c).start()

    @functools.partial(loop, own_steps)
    def _(j):
        for r in range(4):
            guest_copy(r, own_first + j, c).wait_send()
        for r in range(1, 4):
            pass_copy(r, j, flip(c, relations[r])).wait_send()

    for mask in range(1, cells):
        coef_copy(mask, c).wait_send()
    for mask in range(1, cells):
        result_copy(mask, flip(c, mask)).wait_recv()
    first, second = results[opposite_cell], results[other_cell]
    total = total + first[0:1] + second[2:3]
    top = jnp.maximum(jnp.maximum(top, first[1:2]), second[3:4])
    qlive = z * share + lax.broadcasted_iota(jnp.int32, (1, share), 1) < fill
    density[...] = jnp.where(qlive, jnp.log(total), 0.0)
    spread[...] = jnp.where(qlive, jnp.sqrt(top / comps), 0.0)
    for mask in range(1, cells):
        result_copy(mask, c).wait_send()


def by_kernel(counts, loadings, kernel_widths, width_index, block_fill, plan):
    cells, groups = lax.axis_size("cell"), lax.axis_size("gene")
    rows, comps = counts.shape[0], loadings.shape[1]
    share = rows // groups
    steps, own_steps = rows // 2 // PIECE, share // PIECE
    block = pltpu.VMEM((rows, comps), jnp.bfloat16)
    dma = pltpu.SemaphoreType.DMA
    vmem, smem = pl.BlockSpec(memory_space=pltpu.VMEM), pl.BlockSpec(memory_space=pltpu.SMEM)
    out = jax.ShapeDtypeStruct((1, share), jnp.float32)
    density, spread = pl.pallas_call(
        functools.partial(kernel, cells),
        out_shape=(out, out),
        in_specs=[pl.BlockSpec(memory_space=pl.ANY), vmem, vmem, smem, smem, smem],
        out_specs=(vmem, vmem),
        scratch_shapes=[
            pltpu.VMEM(counts.shape, counts.dtype),
            block,
            block,
            block,
            block,
            pltpu.VMEM((cells, share, comps), jnp.bfloat16),
            pltpu.VMEM((cells, 8, share), jnp.float32),
            pltpu.VMEM((8, share), jnp.float32),
            pltpu.VMEM((cells, 8, share), jnp.float32),
            pltpu.VMEM((rows, 128), jnp.float32),
            pltpu.VMEM((rows, 128), jnp.float32),
            dma((2 * steps,)),
            dma((2 * steps,)),
            dma((2 * steps,)),
            dma((steps,)),
            dma((steps,)),
            dma((2 * steps,)),
            dma((2 * steps,)),
            dma((steps,)),
            dma((steps,)),
            dma((4 * own_steps,)),
            dma((4 * own_steps,)),
            dma((3 * own_steps,)),
            dma((3 * own_steps,)),
            dma((cells - 1,)),
            dma((cells - 1,)),
            dma((cells - 1,)),
            dma((cells - 1,)),
        ],
        compiler_params=pltpu.CompilerParams(
            collective_id=0, has_side_effects=True, vmem_limit_bytes=48 * 1024 * 1024
        ),
    )(counts, loadings, width_index.reshape(1, share), kernel_widths, block_fill, plan)
    return density.reshape(share), spread.reshape(share)


def exchange(value, stride, axis):
    cells = lax.axis_size(axis)
    for bit in range(cells.bit_length() - 1):
        pairs = [(source, source ^ (1 << bit)) for source in range(cells)]
        chosen = jnp.bitwise_and(jnp.right_shift(stride, bit), 1) == 1
        value = lax.cond(
            chosen,
            lambda v: jax.tree.map(lambda a: lax.ppermute(a, axis, pairs), v),
            lambda v: v,
            value,
        )
    return value


def block_terms(queries, coef, keys, fill):
    qf = queries.astype(jnp.float32)
    kf = keys.astype(jnp.float32)
    qnorm = jnp.sum(qf * qf, axis=1)
    knorm = jnp.sum(kf * kf, axis=1)
    inner = jnp.einsum("qc,kc->qk", queries, keys, preferred_element_type=jnp.float32)
    dist = jnp.maximum(qnorm[:, None] + knorm[None, :] - 2.0 * inner, 0.0)
    live = jnp.arange(keys.shape[0], dtype=jnp.int32)[None, :] < fill
    kernel = jnp.where(live, jnp.exp(-dist * coef[:, None]), 0.0)
    return (jnp.sum(kernel, axis=1), jnp.max(jnp.where(live, dist, 0.0), axis=1))


def lookup(table, index):
    slots = jnp.arange(table.shape[0], dtype=jnp.int32)
    return jnp.sum(jnp.where(slots == index, table, 0))


def by_exchange(counts, loadings, kernel_widths, width_index, block_fill, plan):
    groups = lax.axis_size("gene")
    share = counts.shape[0] // groups
    gene_pos = lax.axis_index("gene")
    own_fill = lookup(block_fill, lax.axis_index("cell"))
    partial_scores = jnp.dot(counts, loadings, preferred_element_type=jnp.float32)
    mine = lax.psum_scatter(partial_scores, "gene", scatter_dimension=0, tiled=True)
    mine = mine.astype(jnp.bfloat16)
    whole = lax.all_gather(mine, "gene", axis=0, tiled=True)
    comps = whole.shape[1]
    picked = width_index[:, None] == jnp.arange(kernel_widths.shape[0], dtype=jnp.int32)[None, :]
    width = jnp.sum(jnp.where(picked, kernel_widths[None, :], 0.0), axis=1)
    coef = 1.0 / (2.0 * comps * width * width)
    total, top = block_terms(mine, coef, whole, own_fill)
    for step in range(plan.shape[0]):
        guests, guest_coef = exchange((mine, coef), plan[step], "cell")
        terms = block_terms(guests, guest_coef, whole, own_fill)
        more, far = exchange(terms, plan[step], "cell")
        total = total + more
        top = jnp.maximum(top, far)
    positions = gene_pos * share + jnp.arange(share, dtype=jnp.int32)
    qlive = positions < own_fill
    density = jnp.where(qlive, jnp.log(total), 0.0)
    spread = jnp.where(qlive, jnp.sqrt(top / comps), 0.0)
    return (density, spread)


def solution(mesh):
    placed = (P("cell", "gene"), P("gene", None), P(), P(("cell", "gene")), P(), P())
    small = mesh.shape["cell"] == 8 and mesh.shape["gene"] == 4
    return jax.shard_map(
        by_kernel if small else by_exchange,
        mesh=mesh,
        in_specs=placed,
        out_specs=(P(("cell", "gene")), P(("cell", "gene"))),
        check_vma=False,
    )
```

profile of v0, /device:TPU:0, one launch (start us, length us, event | category | flops | bytes accessed | tf_op | source)
XLA Modules:
  0.0 76.1 jit_solution(433096153275054140)
XLA Ops:
  0.6 0.0 copy-start
  0.6 2.2 %copy-done = bf16[2048,1024]{1,0:T(8,128)(2,1)S(1)} copy-done((bf16[2048,1024]{1,0:T(8,128)(2,1)S(1)}, bf16[2048,1024]{1,0:T(8,128)(2,1)}, u32[]{:S(2)}) %copy-start) | copy-done | bytes 4194328
  2.8 0.0 copy-start.1
  2.8 1.0 %copy-done.1 = bf16[1024,256]{1,0:T(8,128)(2,1)S(1)} copy-done((bf16[1024,256]{1,0:T(8,128)(2,1)S(1)}, bf16[1024,256]{1,0:T(8,128)(2,1)}, u32[]{:S(2)}) %copy-start.1) | copy-done | bytes 524312
  3.9 0.0 copy-start.2
  3.9 0.7 copy-done.2
  4.5 0.0 copy-start.3
  4.5 0.7 copy-done.3
  5.2 0.0 copy-start.4
  5.2 0.7 copy-done.4
  5.9 0.0 copy-start.5
  5.9 0.7 copy-done.5
  6.5 68.4 %shard_map.77 = (f32[1,512]{1,0:T(1,128)S(1)}, f32[1,512]{1,0:T(1,128)S(1)}) custom-call(bf16[2048,1024]{1,0:T(8,128)(2,1)S(1)} %copy-done, bf16[1024,256]{1,0:T(8,128)(2,1)S(1)} %copy-done.1, s32[1,512]{1,0:T(1,128)S(1)} %bitcast.3, f32[8]{0:T(128)S(1)} %copy-done.3, s32[8]{0:T(128)S(1)} %copy-done.4, s32[2]{0:T(128)S(1)} %copy-done.5), custom_call_target="tpu_custom_call" | custom-call | tf_op jit(solution)/shard_map/pallas_call | solution.py:335
  74.9 0.6 copy.10
  75.5 0.6 copy.11
Async XLA Ops:
  0.6 2.2 %copy-start = (bf16[2048,1024]{1,0:T(8,128)(2,1)S(1)}, bf16[2048,1024]{1,0:T(8,128)(2,1)}, u32[]{:S(2)}) copy-start(bf16[2048,1024]{1,0:T(8,128)(2,1)} %counts.1) | copy-start | bytes 12582916
  2.8 1.0 %copy-start.1 = (bf16[1024,256]{1,0:T(8,128)(2,1)S(1)}, bf16[1024,256]{1,0:T(8,128)(2,1)}, u32[]{:S(2)}) copy-start(bf16[1024,256]{1,0:T(8,128)(2,1)} %loadings.1) | copy-start | bytes 1572868
  3.9 0.7 copy-start.2
  4.5 0.7 copy-start.3
  5.2 0.7 copy-start.4
  5.9 0.7 copy-start.5
where the time goes:
time: 76.3 us; the launch traced here: 76.1 us
  Pallas kernels  68.4 us (90%)
  local copies, waits for them, and re-layouts  7.03 us (9%)
    pallas_call x1, Pallas kernels, by_kernel(): pl.pallas_call(functools.partial(kernel, cells), out_shape=(out, out), in...  68.4 us
    unnamed x14, local copies, waits for them, and re-layouts  7.03 us

commit v1 on v0

--- a/solution.py
+++ b/solution.py
@@ -29,13 +29,19 @@
 def kernel(
     cells,
     counts,
+    loadings_in,
+    index_in,
+    widths_in,
+    fills_in,
+    plan_in,
+    density,
+    spread,
     loadings,
     index,
     widths,
     fills,
     plan,
-    density,
-    spread,
+    small_sem,
     held,
     wire,
     inbox,
@@ -77,10 +83,12 @@
     mate = z + 1 - 2 * (z % 2)
     opposite = 3 - z
     near, far = side * half, half - side * half
-    own_first = z % 2 * own_steps
     relations = (1, 2, 4, 6)
 
     def part(base, i):
+        return piece(base, i % 2 * own_steps + i // 2)
+
+    def piece(base, i):
         return pl.ds(pl.multiple_of(base + i * PIECE, PIECE), PIECE)
 
     def held_copy(base, i, k):
@@ -104,17 +112,17 @@
         return remote(whole.at[at], whole.at[at], over_send.at[i], over_recv.at[i], gene=opposite)
 
     def guest_copy(r, i, slot):
-        j = i - own_first
+        j = i // 2
         return remote(
             whole.at[part(near, i)],
-            guests.at[slot, part(0, j)],
+            guests.at[slot, piece(0, j)],
             guest_send.at[r * own_steps + j],
             guest_recv.at[r * own_steps + j],
             cell=flip(c, relations[r]),
         )
 
     def pass_copy(r, j, slot):
-        at = part(0, j)
+        at = piece(0, j)
         return remote(
             guests.at[slot, at],
             guests.at[slot, at],
@@ -134,7 +142,7 @@
         )
 
     def offer(i):
-        @pl.when((i >= own_first) & (i < own_first + own_steps))
+        @pl.when(i % 2 == z % 2)
         def _():
             for r in range(4):
                 guest_copy(r, i, c).start()
@@ -142,6 +150,15 @@
     def product(base, i, k):
         held_copy(base, i, k).wait()
         return jnp.dot(held[part(base, i), :], loadings[...], preferred_element_type=jnp.float32)
+
+    def norms(base, i):
+        at = part(base, i)
+        keys = whole[at, :].astype(jnp.float32)
+        norm = jnp.sum(keys * keys, axis=1, keepdims=True)
+        first = base + (i % 2 * own_steps + i // 2) * PIECE
+        live = first + lax.broadcasted_iota(jnp.int32, (PIECE, 1), 0) < fill
+        near_norm[at, :] = jnp.broadcast_to(jnp.where(live, norm, FAR), (PIECE, 128))
+        far_norm[at, :] = jnp.broadcast_to(jnp.where(live, norm, -FAR), (PIECE, 128))
 
     def loop(count, body):
         def step(i, carry):
@@ -150,10 +167,28 @@
 
         lax.fori_loop(0, count, step, 0)
 
-    @functools.partial(loop, steps)
+    small = [
+        pltpu.make_async_copy(source, target, small_sem.at[k])
+        for k, (source, target) in enumerate(
+            (
+                (loadings_in, loadings),
+                (index_in, index),
+                (widths_in, widths),
+                (fills_in, fills),
+                (plan_in, plan),
+            )
+        )
+    ]
+    small[0].start()
+    held_copy(far, 0, 0).start()
+    held_copy(near, 0, 1).start()
+    for copy in small[1:]:
+        copy.start()
+
+    @functools.partial(loop, steps - 1)
     def _(i):
-        held_copy(far, i, 0).start()
-        held_copy(near, i, 1).start()
+        held_copy(far, i + 1, 0).start()
+        held_copy(near, i + 1, 1).start()
 
     barrier = pltpu.get_barrier_semaphore()
     for mask in range(1, cells):
@@ -164,6 +199,9 @@
     def _():
         pl.semaphore_signal(barrier, inc=1, device_id={"gene": opposite}, device_id_type=MESH)
 
+    for copy in small:
+        copy.wait()
+    fill = fills[c]
     picked = jnp.zeros(index.shape, jnp.float32)
     for entry in range(widths.shape[0]):
         picked = picked + jnp.where(index[...] == entry, widths[entry], 0.0)
@@ -187,7 +225,9 @@
         def _(i):
             final_copy(near, i, 1).wait_recv()
             offer(i)
+            norms(near, i)
             final_copy(far, i, 0).wait_recv()
+            norms(far, i)
 
         @functools.partial(loop, steps)
         def _(i):
@@ -200,31 +240,34 @@
         for mask in range(1, cells):
             coef_copy(mask, c).start()
 
-        @functools.partial(loop, steps)
+        @functools.partial(loop, steps + 2)
         def _(i):
-            far_part = product(far, i, 0)
-            near_part = product(near, i, 1)
-            end_copy(far, i, 0).wait_recv()
-            far_part = far_part + inbox[part(far, i), :].astype(jnp.float32)
-            wire[part(far, i), :] = far_part.astype(wire.dtype)
-            mid_copy(far, i).start()
-
-            @pl.when(i > 0)
+            @pl.when(i < steps)
             def _():
-                over_copy(far, i - 1).wait_recv()
-                final_copy(far, i - 1, 0).start()
-
-            end_copy(near, i, 1).wait_recv()
-            near_part = near_part + inbox[part(near, i), :].astype(jnp.float32)
-            mid_copy(near, i).wait_recv()
-            near_part = near_part + cross[part(near, i), :].astype(jnp.float32)
-            whole[part(near, i), :] = near_part.astype(whole.dtype)
-            over_copy(near, i).start()
-            final_copy(near, i, 1).start()
-            offer(i)
-
-        over_copy(far, steps - 1).wait_recv()
-        final_copy(far, steps - 1, 0).start()
+                total = product(far, i, 0)
+                end_copy(far, i, 0).wait_recv()
+                total = total + inbox[part(far, i), :].astype(jnp.float32)
+                wire[part(far, i), :] = total.astype(wire.dtype)
+                mid_copy(far, i).start()
+
+            @pl.when(i >= 2)
+            def _():
+                over_copy(far, i - 2).wait_recv()
+                final_copy(far, i - 2, 0).start()
+                norms(far, i - 2)
+
+            @pl.when((i >= 1) & (i <= steps))
+            def _():
+                total = product(near, i - 1, 1)
+                end_copy(near, i - 1, 1).wait_recv()
+                total = total + inbox[part(near, i - 1), :].astype(jnp.float32)
+                mid_copy(near, i - 1).wait_recv()
+                total = total + cross[part(near, i - 1), :].astype(jnp.float32)
+                whole[part(near, i - 1), :] = total.astype(whole.dtype)
+                over_copy(near, i - 1).start()
+                final_copy(near, i - 1, 1).start()
+                offer(i - 1)
+                norms(near, i - 1)
 
         @functools.partial(loop, steps)
         def _(i):
@@ -237,19 +280,8 @@
     def _(j):
         for r in range(1, 4):
             slot = flip(c, relations[r])
-            guest_copy(r, own_first + j, slot).wait_recv()
+            guest_copy(r, 2 * j + z % 2, slot).wait_recv()
             pass_copy(r, j, slot).start()
-
-    fill = fills[c]
-
-    @functools.partial(loop, rows // TILE)
-    def _(t):
-        at = pl.ds(pl.multiple_of(t * TILE, TILE), TILE)
-        keys = whole[at, :].astype(jnp.float32)
-        norm = jnp.sum(keys * keys, axis=1, keepdims=True)
-        live = t * TILE + lax.broadcasted_iota(jnp.int32, (TILE, 1), 0) < fill
-        near_norm[at, :] = jnp.broadcast_to(jnp.where(live, norm, FAR), (TILE, 128))
-        far_norm[at, :] = jnp.broadcast_to(jnp.where(live, norm, -FAR), (TILE, 128))
 
     def dot_t(a, b):
         return lax.dot_general(a, b, (((1,), (1,)), ((), ())), preferred_element_type=jnp.float32)
@@ -285,7 +317,7 @@
 
     @functools.partial(loop, own_steps)
     def _(j):
-        guest_copy(0, own_first + j, flip(c, 1)).wait_recv()
+        guest_copy(0, 2 * j + z % 2, flip(c, 1)).wait_recv()
         for r in range(1, 4):
             pass_copy(r, j, flip(c, relations[r] + 1)).wait_recv()
 
@@ -305,7 +337,7 @@
     @functools.partial(loop, own_steps)
     def _(j):
         for r in range(4):
-            guest_copy(r, own_first + j, c).wait_send()
+            guest_copy(r, 2 * j + z % 2, c).wait_send()
         for r in range(1, 4):
             pass_copy(r, j, flip(c, relations[r])).wait_send()
 
@@ -330,14 +362,20 @@
     steps, own_steps = rows // 2 // PIECE, share // PIECE
     block = pltpu.VMEM((rows, comps), jnp.bfloat16)
     dma = pltpu.SemaphoreType.DMA
-    vmem, smem = pl.BlockSpec(memory_space=pltpu.VMEM), pl.BlockSpec(memory_space=pltpu.SMEM)
+    vmem = pl.BlockSpec(memory_space=pltpu.VMEM)
     out = jax.ShapeDtypeStruct((1, share), jnp.float32)
     density, spread = pl.pallas_call(
         functools.partial(kernel, cells),
         out_shape=(out, out),
-        in_specs=[pl.BlockSpec(memory_space=pl.ANY), vmem, vmem, smem, smem, smem],
+        in_specs=[pl.BlockSpec(memory_space=pltpu.HBM)] * 6,
         out_specs=(vmem, vmem),
         scratch_shapes=[
+            pltpu.VMEM(loadings.shape, loadings.dtype),
+            pltpu.VMEM((1, share), width_index.dtype),
+            pltpu.SMEM(kernel_widths.shape, kernel_widths.dtype),
+            pltpu.SMEM(block_fill.shape, block_fill.dtype),
+            pltpu.SMEM(plan.shape, plan.dtype),
+            dma((5,)),
             pltpu.VMEM(counts.shape, counts.dtype),
             block,
             block,
@@ -368,7 +406,7 @@
             dma((cells - 1,)),
         ],
         compiler_params=pltpu.CompilerParams(
-            collective_id=0, has_side_effects=True, vmem_limit_bytes=48 * 1024 * 1024
+            collective_id=0, has_side_effects=True, vmem_limit_bytes=63 * 1024 * 1024
         ),
     )(counts, loadings, width_index.reshape(1, share), kernel_widths, block_fill, plan)
     return density.reshape(share), spread.reshape(share)

time: 76.3 us -> 65.5 us (0.86)
  Pallas kernels: 68.4 us -> 62.2 us
  local copies, waits for them, and re-layouts: 7.03 us -> 2.48 us
    pallas_call x1, Pallas kernels: 68.4 us -> 62.2 us  [by_kernel(): pl.pallas_call(functools.partial(kernel, cells), out_shape=(out, out), in...]
    unnamed x14 -> x2, local copies, waits for them, and re-layouts: 7.03 us -> 2.48 us
where the time goes in v1:
time: 65.5 us; the launch traced here: 65.3 us
  Pallas kernels  62.2 us (95%)
  local copies, waits for them, and re-layouts  2.48 us (4%)
    pallas_call x1, Pallas kernels, by_kernel(): pl.pallas_call(functools.partial(kernel, cells), out_shape=(out, out), in...  62.2 us
    unnamed x2, local copies, waits for them, and re-layouts  2.48 us

profile of v1, /device:TPU:0, one launch (start us, length us, event | category | flops | bytes accessed | tf_op | source)
XLA Modules:
  0.0 65.3 jit_solution(14060876081811418250)
XLA Ops:
  0.6 62.2 %shard_map.77 = (f32[1,512]{1,0:T(1,128)}, f32[1,512]{1,0:T(1,128)}) custom-call(bf16[2048,1024]{1,0:T(8,128)(2,1)} %counts.1, bf16[1024,256]{1,0:T(8,128)(2,1)} %loadings_in.1, s32[1,512]{1,0:T(1,128)} %bitcast.3, f32[8]{0:T(128)} %widths_in.1, s32[8]{0:T(128)} %fills_in.1, s32[2]{0:T(128)} %plan_in.1), custom_call_target="tpu_custom_call" | custom-call | tf_op jit(solution)/shard_map/pallas_call | solution.py:367
  62.8 1.2 %copy.10 = f32[512]{0:T(512)} copy(f32[512]{0:T(512)} %bitcast.5) | data formatting | bytes 4096
  64.1 1.2 %copy.11 = f32[512]{0:T(512)} copy(f32[512]{0:T(512)} %bitcast.4) | data formatting | bytes 4096

commit v2 on v1

--- a/solution.py
+++ b/solution.py
@@ -53,6 +53,9 @@
     results,
     near_norm,
     far_norm,
+    turned_queries,
+    even,
+    odd,
     held_sem,
     end_send,
     end_recv,
@@ -276,44 +279,50 @@
             final_copy(near, i, 1).wait_send()
             final_copy(far, i, 0).wait_send()
 
-    @functools.partial(loop, own_steps)
-    def _(j):
+    def forward(j):
         for r in range(1, 4):
             slot = flip(c, relations[r])
             guest_copy(r, 2 * j + z % 2, slot).wait_recv()
             pass_copy(r, j, slot).start()
 
-    def dot_t(a, b):
-        return lax.dot_general(a, b, (((1,), (1,)), ((), ())), preferred_element_type=jnp.float32)
+    loop(own_steps - 1, forward)
 
     def terms(queries, coef):
-        square = queries.astype(jnp.float32)
-        square = square * square
-        high = square.astype(jnp.bfloat16)
-        low = (square - high.astype(jnp.float32)).astype(jnp.bfloat16)
-        ones = jnp.ones((8, comps), jnp.bfloat16)
-        norm = dot_t(ones, high) + dot_t(ones, low)
+        turned = queries.astype(jnp.float32).T
+        norm = jnp.broadcast_to(jnp.sum(turned * turned, axis=0, keepdims=True), (8, share))
+        turned_queries[...] = (turned * -2.0).astype(turned_queries.dtype)
         rate = coef * (-1.0 / math.log(2.0))
-        doubled = queries * jnp.asarray(-2.0, queries.dtype)
+        tiles = rows // TILE
+
+        def multiply(t, target):
+            at = pl.ds(pl.multiple_of(t * TILE, TILE), TILE)
+            target[...] = jnp.dot(whole[at, :], turned_queries[...], preferred_element_type=jnp.float32)
+
+        def collect(t, source, total, top):
+            for group in range(TILE // 8):
+                at = pl.ds(pl.multiple_of(t * TILE + group * 8, 8), 8)
+                base = source[group * 8 : group * 8 + 8, :] + norm
+                closest = jnp.concatenate([near_norm[at, :]] * (share // 128), axis=1)
+                farthest = jnp.concatenate([far_norm[at, :]] * (share // 128), axis=1)
+                total = total + jnp.exp2(jnp.maximum(base + closest, 0.0) * rate)
+                top = jnp.maximum(top, base + farthest)
+            return total, top
 
         def step(t, carry):
             total, top = carry
-            at = pl.ds(pl.multiple_of(t * TILE, TILE), TILE)
-            inner = dot_t(whole[at, :], doubled).reshape(TILE // 8, 8, share)
-            closest = jnp.concatenate([near_norm[at, :].reshape(TILE // 8, 8, 128)] * (share // 128), axis=2)
-            farthest = jnp.concatenate([far_norm[at, :].reshape(TILE // 8, 8, 128)] * (share // 128), axis=2)
-            base = inner + norm[None]
-            weight = jnp.exp2(jnp.maximum(base + closest, 0.0) * rate[None])
-            total = total + jnp.sum(weight, axis=0)
-            top = jnp.maximum(top, jnp.max(base + farthest, axis=0))
-            return total, top
+            multiply(2 * t + 1, odd)
+            total, top = collect(2 * t, even, total, top)
+            multiply(jnp.minimum(2 * t + 2, tiles - 1), even)
+            return collect(2 * t + 1, odd, total, top)
 
         zero = jnp.zeros((8, share), jnp.float32)
-        total, top = lax.fori_loop(0, rows // TILE, step, (zero, zero))
+        multiply(0, even)
+        total, top = lax.fori_loop(0, tiles // 2, step, (zero, zero))
         return jnp.sum(total, axis=0, keepdims=True), jnp.max(top, axis=0, keepdims=True)
 
     own_rows = pl.ds(pl.multiple_of(z * share, share), share)
     total, top = terms(whole[own_rows, :], coefs[c])
+    forward(own_steps - 1)
 
     @functools.partial(loop, own_steps)
     def _(j):
@@ -387,6 +396,9 @@
             pltpu.VMEM((cells, 8, share), jnp.float32),
             pltpu.VMEM((rows, 128), jnp.float32),
             pltpu.VMEM((rows, 128), jnp.float32),
+            pltpu.VMEM((comps, share), jnp.bfloat16),
+            pltpu.VMEM((TILE, share), jnp.float32),
+            pltpu.VMEM((TILE, share), jnp.float32),
             dma((2 * steps,)),
             dma((2 * steps,)),
             dma((2 * steps,)),

time: 65.5 us -> 63.3 us (0.966)
  Pallas kernels: 62.2 us -> 60 us
    pallas_call x1, Pallas kernels: 62.2 us -> 60 us  [by_kernel(): pl.pallas_call(functools.partial(kernel, cells), out_shape=(out, out), in...]
where the time goes in v2:
time: 63.3 us; the launch traced here: 63.1 us
  Pallas kernels  60 us (95%)
  local copies, waits for them, and re-layouts  2.48 us (4%)
  between operations  0.64 us (1%)
    pallas_call x1, Pallas kernels, by_kernel(): pl.pallas_call(functools.partial(kernel, cells), out_shape=(out, out), in...  60 us
    unnamed x2, local copies, waits for them, and re-layouts  2.48 us

profile of v2, /device:TPU:0, one launch (start us, length us, event | category | flops | bytes accessed | tf_op | source)
XLA Modules:
  0.0 63.1 jit_solution(285921004559238218)
XLA Ops:
  0.6 60.0 %shard_map.77 = (f32[1,512]{1,0:T(1,128)}, f32[1,512]{1,0:T(1,128)}) custom-call(bf16[2048,1024]{1,0:T(8,128)(2,1)} %counts.1, bf16[1024,256]{1,0:T(8,128)(2,1)} %loadings_in.1, s32[1,512]{1,0:T(1,128)} %bitcast.3, f32[8]{0:T(128)} %widths_in.1, s32[8]{0:T(128)} %fills_in.1, s32[2]{0:T(128)} %plan_in.1), custom_call_target="tpu_custom_call" | custom-call | tf_op jit(solution)/shard_map/pallas_call | solution.py:376
  60.6 1.2 %copy.10 = f32[512]{0:T(512)} copy(f32[512]{0:T(512)} %bitcast.5) | data formatting | bytes 4096
  61.8 1.2 %copy.11 = f32[512]{0:T(512)} copy(f32[512]{0:T(512)} %bitcast.4) | data formatting | bytes 4096

commit v3 on v2

--- a/solution.py
+++ b/solution.py
@@ -27,20 +27,18 @@
 
 
 def kernel(
-    cells,
+    masks,
     counts,
     loadings_in,
     index_in,
     widths_in,
     fills_in,
-    plan_in,
     density,
     spread,
     loadings,
     index,
     widths,
     fills,
-    plan,
     small_sem,
     held,
     wire,
@@ -67,8 +65,6 @@
     over_recv,
     guest_send,
     guest_recv,
-    pass_send,
-    pass_recv,
     coef_send,
     coef_recv,
     result_send,
@@ -86,7 +82,6 @@
     mate = z + 1 - 2 * (z % 2)
     opposite = 3 - z
     near, far = side * half, half - side * half
-    relations = (1, 2, 4, 6)
 
     def part(base, i):
         return piece(base, i % 2 * own_steps + i // 2)
@@ -114,41 +109,27 @@
         at = part(base, i)
         return remote(whole.at[at], whole.at[at], over_send.at[i], over_recv.at[i], gene=opposite)
 
-    def guest_copy(r, i, slot):
+    def guest_copy(r, i):
         j = i // 2
         return remote(
             whole.at[part(near, i)],
-            guests.at[slot, piece(0, j)],
+            guests.at[r, piece(0, j)],
             guest_send.at[r * own_steps + j],
             guest_recv.at[r * own_steps + j],
-            cell=flip(c, relations[r]),
+            cell=flip(c, masks[r]),
         )
 
-    def pass_copy(r, j, slot):
-        at = piece(0, j)
-        return remote(
-            guests.at[slot, at],
-            guests.at[slot, at],
-            pass_send.at[(r - 1) * own_steps + j],
-            pass_recv.at[(r - 1) * own_steps + j],
-            cell=flip(c, 1),
-        )
-
-    def coef_copy(mask, slot):
-        return remote(
-            coefs.at[slot], coefs.at[slot], coef_send.at[mask - 1], coef_recv.at[mask - 1], cell=flip(c, mask)
-        )
-
-    def result_copy(mask, slot):
-        return remote(
-            outbox, results.at[slot], result_send.at[mask - 1], result_recv.at[mask - 1], cell=flip(c, mask)
-        )
+    def coef_copy(r):
+        return remote(coefs.at[2], coefs.at[r], coef_send.at[r], coef_recv.at[r], cell=flip(c, masks[r]))
+
+    def result_copy(r):
+        return remote(outbox.at[r], results.at[r], result_send.at[r], result_recv.at[r], cell=flip(c, masks[r]))
 
     def offer(i):
         @pl.when(i % 2 == z % 2)
         def _():
-            for r in range(4):
-                guest_copy(r, i, c).start()
+            for r in range(2):
+                guest_copy(r, i).start()
 
     def product(base, i, k):
         held_copy(base, i, k).wait()
@@ -178,7 +159,6 @@
                 (index_in, index),
                 (widths_in, widths),
                 (fills_in, fills),
-                (plan_in, plan),
             )
         )
     ]
@@ -194,7 +174,7 @@
         held_copy(near, i + 1, 1).start()
 
     barrier = pltpu.get_barrier_semaphore()
-    for mask in range(1, cells):
+    for mask in masks:
         pl.semaphore_signal(barrier, inc=1, device_id={"cell": flip(c, mask)}, device_id_type=MESH)
     pl.semaphore_signal(barrier, inc=1, device_id={"gene": mate}, device_id_type=MESH)
 
@@ -209,11 +189,11 @@
     for entry in range(widths.shape[0]):
         picked = picked + jnp.where(index[...] == entry, widths[entry], 0.0)
     own_coef = 1.0 / (2.0 * comps * picked * picked)
-    coefs[c] = jnp.broadcast_to(own_coef, (8, share))
+    coefs[2] = jnp.broadcast_to(own_coef, (8, share))
 
     @pl.when(is_end)
     def _():
-        pl.semaphore_wait(barrier, cells)
+        pl.semaphore_wait(barrier, 3)
 
         @functools.partial(loop, steps)
         def _(i):
@@ -221,8 +201,8 @@
                 wire[part(base, i), :] = product(base, i, k).astype(wire.dtype)
                 end_copy(base, i, k).start()
 
-        for mask in range(1, cells):
-            coef_copy(mask, c).start()
+        for r in range(2):
+            coef_copy(r).start()
 
         @functools.partial(loop, steps)
         def _(i):
@@ -239,9 +219,9 @@
 
     @pl.when(is_mid)
     def _():
-        pl.semaphore_wait(barrier, cells + 1)
-        for mask in range(1, cells):
-            coef_copy(mask, c).start()
+        pl.semaphore_wait(barrier, 4)
+        for r in range(2):
+            coef_copy(r).start()
 
         @functools.partial(loop, steps + 2)
         def _(i):
@@ -279,14 +259,6 @@
             final_copy(near, i, 1).wait_send()
             final_copy(far, i, 0).wait_send()
 
-    def forward(j):
-        for r in range(1, 4):
-            slot = flip(c, relations[r])
-            guest_copy(r, 2 * j + z % 2, slot).wait_recv()
-            pass_copy(r, j, slot).start()
-
-    loop(own_steps - 1, forward)
-
     def terms(queries, coef):
         turned = queries.astype(jnp.float32).T
         norm = jnp.broadcast_to(jnp.sum(turned * turned, axis=0, keepdims=True), (8, share))
@@ -321,47 +293,34 @@
         return jnp.sum(total, axis=0, keepdims=True), jnp.max(top, axis=0, keepdims=True)
 
     own_rows = pl.ds(pl.multiple_of(z * share, share), share)
-    total, top = terms(whole[own_rows, :], coefs[c])
-    forward(own_steps - 1)
+    total, top = terms(whole[own_rows, :], coefs[2])
+    for r in (1, 0):
+
+        @functools.partial(loop, own_steps)
+        def _(j):
+            guest_copy(r, 2 * j + z % 2).wait_recv()
+
+        coef_copy(r).wait_recv()
+        more, most = terms(guests[r], coefs[r])
+        outbox[r] = jnp.concatenate([more, most, jnp.zeros((6, share), jnp.float32)], axis=0)
+        result_copy(r).start()
 
     @functools.partial(loop, own_steps)
     def _(j):
-        guest_copy(0, 2 * j + z % 2, flip(c, 1)).wait_recv()
-        for r in range(1, 4):
-            pass_copy(r, j, flip(c, relations[r] + 1)).wait_recv()
-
-    for mask in range(1, cells):
-        coef_copy(mask, flip(c, mask)).wait_recv()
-
-    opposite_cell = flip(c, cells - 1)
-    other_cell = jnp.bitwise_and(jnp.bitwise_xor(c, plan[0] + plan[1] - (cells - 1)), cells - 1)
-    for at, guest in ((0, opposite_cell), (2, other_cell)):
-        more, most = terms(guests[guest], coefs[guest])
-        outbox[at : at + 1, :] = more
-        outbox[at + 1 : at + 2, :] = most
-    outbox[4:8, :] = jnp.zeros((4, share), jnp.float32)
-    for mask in range(1, cells):
-        result_copy(mask, c).start()
-
-    @functools.partial(loop, own_steps)
-    def _(j):
-        for r in range(4):
-            guest_copy(r, 2 * j + z % 2, c).wait_send()
-        for r in range(1, 4):
-            pass_copy(r, j, flip(c, relations[r])).wait_send()
-
-    for mask in range(1, cells):
-        coef_copy(mask, c).wait_send()
-    for mask in range(1, cells):
-        result_copy(mask, flip(c, mask)).wait_recv()
-    first, second = results[opposite_cell], results[other_cell]
-    total = total + first[0:1] + second[2:3]
-    top = jnp.maximum(jnp.maximum(top, first[1:2]), second[3:4])
+        for r in range(2):
+            guest_copy(r, 2 * j + z % 2).wait_send()
+
+    for r in (1, 0):
+        coef_copy(r).wait_send()
+        result_copy(r).wait_recv()
+        back = results[r]
+        total = total + back[0:1]
+        top = jnp.maximum(top, back[1:2])
     qlive = z * share + lax.broadcasted_iota(jnp.int32, (1, share), 1) < fill
     density[...] = jnp.where(qlive, jnp.log(total), 0.0)
     spread[...] = jnp.where(qlive, jnp.sqrt(top / comps), 0.0)
-    for mask in range(1, cells):
-        result_copy(mask, c).wait_send()
+    for r in range(2):
+        result_copy(r).wait_send()
 
 
 def by_kernel(counts, loadings, kernel_widths, width_index, block_fill, plan):
@@ -373,54 +332,57 @@
     dma = pltpu.SemaphoreType.DMA
     vmem = pl.BlockSpec(memory_space=pltpu.VMEM)
     out = jax.ShapeDtypeStruct((1, share), jnp.float32)
-    density, spread = pl.pallas_call(
-        functools.partial(kernel, cells),
-        out_shape=(out, out),
-        in_specs=[pl.BlockSpec(memory_space=pltpu.HBM)] * 6,
-        out_specs=(vmem, vmem),
-        scratch_shapes=[
-            pltpu.VMEM(loadings.shape, loadings.dtype),
-            pltpu.VMEM((1, share), width_index.dtype),
-            pltpu.SMEM(kernel_widths.shape, kernel_widths.dtype),
-            pltpu.SMEM(block_fill.shape, block_fill.dtype),
-            pltpu.SMEM(plan.shape, plan.dtype),
-            dma((5,)),
-            pltpu.VMEM(counts.shape, counts.dtype),
-            block,
-            block,
-            block,
-            block,
-            pltpu.VMEM((cells, share, comps), jnp.bfloat16),
-            pltpu.VMEM((cells, 8, share), jnp.float32),
-            pltpu.VMEM((8, share), jnp.float32),
-            pltpu.VMEM((cells, 8, share), jnp.float32),
-            pltpu.VMEM((rows, 128), jnp.float32),
-            pltpu.VMEM((rows, 128), jnp.float32),
-            pltpu.VMEM((comps, share), jnp.bfloat16),
-            pltpu.VMEM((TILE, share), jnp.float32),
-            pltpu.VMEM((TILE, share), jnp.float32),
-            dma((2 * steps,)),
-            dma((2 * steps,)),
-            dma((2 * steps,)),
-            dma((steps,)),
-            dma((steps,)),
-            dma((2 * steps,)),
-            dma((2 * steps,)),
-            dma((steps,)),
-            dma((steps,)),
-            dma((4 * own_steps,)),
-            dma((4 * own_steps,)),
-            dma((3 * own_steps,)),
-            dma((3 * own_steps,)),
-            dma((cells - 1,)),
-            dma((cells - 1,)),
-            dma((cells - 1,)),
-            dma((cells - 1,)),
-        ],
-        compiler_params=pltpu.CompilerParams(
-            collective_id=0, has_side_effects=True, vmem_limit_bytes=63 * 1024 * 1024
-        ),
-    )(counts, loadings, width_index.reshape(1, share), kernel_widths, block_fill, plan)
+
+    def call(other):
+        return pl.pallas_call(
+            functools.partial(kernel, (cells - 1, other)),
+            out_shape=(out, out),
+            in_specs=[pl.BlockSpec(memory_space=pltpu.HBM)] * 5,
+            out_specs=(vmem, vmem),
+            scratch_shapes=[
+                pltpu.VMEM(loadings.shape, loadings.dtype),
+                pltpu.VMEM((1, share), width_index.dtype),
+                pltpu.SMEM(kernel_widths.shape, kernel_widths.dtype),
+                pltpu.SMEM(block_fill.shape, block_fill.dtype),
+                dma((4,)),
+                pltpu.VMEM(counts.shape, counts.dtype),
+                block,
+                block,
+                block,
+                block,
+                pltpu.VMEM((2, share, comps), jnp.bfloat16),
+                pltpu.VMEM((3, 8, share), jnp.float32),
+                pltpu.VMEM((2, 8, share), jnp.float32),
+                pltpu.VMEM((2, 8, share), jnp.float32),
+                pltpu.VMEM((rows, 128), jnp.float32),
+                pltpu.VMEM((rows, 128), jnp.float32),
+                pltpu.VMEM((comps, share), jnp.bfloat16),
+                pltpu.VMEM((TILE, share), jnp.float32),
+                pltpu.VMEM((TILE, share), jnp.float32),
+                dma((2 * steps,)),
+                dma((2 * steps,)),
+                dma((2 * steps,)),
+                dma((steps,)),
+                dma((steps,)),
+                dma((2 * steps,)),
+                dma((2 * steps,)),
+                dma((steps,)),
+                dma((steps,)),
+                dma((2 * own_steps,)),
+                dma((2 * own_steps,)),
+                dma((2,)),
+                dma((2,)),
+                dma((2,)),
+                dma((2,)),
+            ],
+            compiler_params=pltpu.CompilerParams(
+                collective_id=other - 1, has_side_effects=True, vmem_limit_bytes=63 * 1024 * 1024
+            ),
+        )
+
+    arrays = (counts, loadings, width_index.reshape(1, share), kernel_widths, block_fill)
+    other = plan[0] + plan[1] - (cells - 1)
+    density, spread = lax.switch(other - 1, [call(mask) for mask in range(1, cells - 1)], *arrays)
     return density.reshape(share), spread.reshape(share)
 
 

time: 63.3 us -> 60.5 us (0.956)
  Pallas kernels: 60 us -> 55.5 us
  between operations: 0.64 us -> 1.94 us
    pallas_call x1, Pallas kernels: 60 us -> 55.5 us  [by_kernel(): lax.switch(other - 1, [call(mask) for mask in range(1, cells - 1)], *arrays)]
    unnamed x2, local copies, waits for them, and re-layouts: 2.48 us -> 1.16 us
    slice x0 -> x1, local copies, waits for them, and re-layouts: none -> 1.31 us  [by_kernel(): other = plan[0] + plan[1] - (cells - 1)]
where the time goes in v3:
time: 60.5 us; the launch traced here: 60.2 us
  Pallas kernels  55.5 us (92%)
  local copies, waits for them, and re-layouts  2.47 us (4%)
  between operations  1.94 us (3%)
    pallas_call x1, Pallas kernels, by_kernel(): lax.switch(other - 1, [call(mask) for mask in range(1, cells - 1)], *arrays)  55.5 us
    slice x1, local copies, waits for them, and re-layouts, by_kernel(): other = plan[0] + plan[1] - (cells - 1)  1.31 us

profile of v3, /device:TPU:0, one launch (start us, length us, event | category | flops | bytes accessed | tf_op | source)
XLA Modules:
  0.0 60.2 jit_solution(1511494588425467556)
XLA Ops:
  0.6 1.3 %fusion = (s32[1]{0:T(128)}, s32[1]{0:T(128)}) fusion(s32[2]{0:T(128)} %param.17), kind=kLoop, calls=%fused_computation | loop fusion | bytes 16 | tf_op jit(solution)/shard_map/slice | solution.py:384
  3.2 55.8 %conditional.1 = ((f32[1,512]{1,0:T(1,128)S(1)}, f32[1,512]{1,0:T(1,128)S(1)})) conditional(s32[]{:T(128)} %bitcast, (bf16[2048,1024]{1,0:T(8,128)(2,1)}, bf16[1024,256]{1,0:T(8,128)(2,1)}, s32[1,512]{1,0:T(1,128)}, f32[8]{0:T(128)}, s32[8]{0:T(128)}) %tuple.66, (bf16[2048,1024]{1,0:T(8,128)(2,1)}, ...), branch_computations={%region_0.0_spmd, %region_1.0_spmd, %region_2.0_spmd, %region_3.0_... | conditional | bytes 8 | solution.py:385
  3.3 55.5 %branch_0_fun.1 = (f32[1,512]{1,0:T(1,128)S(1)}, f32[1,512]{1,0:T(1,128)S(1)}) custom-call(bf16[2048,1024]{1,0:T(8,128)(2,1)} %get-tuple-element.74.counts, bf16[1024,256]{1,0:T(8,128)(2,1)} %get-tuple-element.75.loadings_in, s32[1,512]{1,0:T(1,128)} %get-tuple-element.76.index_in, f32[8]{0:T(128)} %get-tuple-element.77.widths_in, s32[8]{0:T(128)} %get-tuple-element.78.fills_in), custom_call_target="tpu_custom_call" | custom-call | tf_op jit(solution)/shard_map/cond/branch_0_fun/pallas_call | solution.py:385
  59.0 0.6 copy.22
  59.6 0.6 copy.23

commit v4 on v2

--- a/solution.py
+++ b/solution.py
@@ -8,7 +8,7 @@
 from jax.sharding import PartitionSpec as P
 
 MESH = pl.DeviceIdType.MESH
-PIECE = 128
+PIECE = 256
 TILE = 256
 FAR = 1e30
 

time: 63.3 us -> 59.2 us (0.935)
  Pallas kernels: 60 us -> 55.9 us
    pallas_call x1, Pallas kernels: 60 us -> 55.9 us  [by_kernel(): pl.pallas_call(functools.partial(kernel, cells), out_shape=(out, out), in...]
where the time goes in v4:
time: 59.2 us; the launch traced here: 59 us
  Pallas kernels  55.9 us (94%)
  local copies, waits for them, and re-layouts  2.48 us (4%)
  between operations  0.64 us (1%)
    pallas_call x1, Pallas kernels, by_kernel(): pl.pallas_call(functools.partial(kernel, cells), out_shape=(out, out), in...  55.9 us
    unnamed x2, local copies, waits for them, and re-layouts  2.48 us

profile of v4, /device:TPU:0, one launch (start us, length us, event | category | flops | bytes accessed | tf_op | source)
XLA Modules:
  0.0 59.0 jit_solution(5195691629877305528)
XLA Ops:
  0.6 55.9 %shard_map.77 = (f32[1,512]{1,0:T(1,128)}, f32[1,512]{1,0:T(1,128)}) custom-call(bf16[2048,1024]{1,0:T(8,128)(2,1)} %counts.1, bf16[1024,256]{1,0:T(8,128)(2,1)} %loadings_in.1, s32[1,512]{1,0:T(1,128)} %bitcast.3, f32[8]{0:T(128)} %widths_in.1, s32[8]{0:T(128)} %fills_in.1, s32[2]{0:T(128)} %plan_in.1), custom_call_target="tpu_custom_call" | custom-call | tf_op jit(solution)/shard_map/pallas_call | solution.py:376
  56.5 1.2 %copy.10 = f32[512]{0:T(512)} copy(f32[512]{0:T(512)} %bitcast.5) | data formatting | bytes 4096
  57.8 1.2 %copy.11 = f32[512]{0:T(512)} copy(f32[512]{0:T(512)} %bitcast.4) | data formatting | bytes 4096
